TPU v7x, 32 devices: a whole 2x2x4 slice. The times are simulated.
32 devices in a mesh: ctx: 8 (over y, x, core), head: 4 (over z).
Axes of the slice: x: 2, y: 2, z: 4, core: 2. Of those that a mesh axis runs over, the one named last changes fastest.
Arguments:
- q_att: bfloat16 [2048, 512], P('ctx', 'head'), may hold values from -6 to 6
- k_att: bfloat16 [2048, 512], P('ctx', 'head'), may hold values from -6 to 6
- v_att: bfloat16 [2048, 512], P('ctx', 'head'), may hold values from -6 to 6
- norm_gain: float32 [512], P('head'), may hold values from 0.25 to 1.75
- hy_q: bfloat16 [2048, 512], P('ctx', 'head'), may hold values from -6 to 6
- hy_k: bfloat16 [2048, 512], P('ctx', 'head'), may hold values from -6 to 6
- feat_w: float32 [3, 7, 512], P(None, None, 'head'), may hold values from -2 to 2
- mr_filt: float32 [128, 32], P(None, 'head'), may hold values from -0.5 to 0.5
- cotangent: bfloat16 [2048, 512], P('ctx', 'head'), may hold values from -6 to 6
Outputs:
- output: bfloat16 [2048, 512], P('ctx', 'head')
- grad_q: bfloat16 [2048, 512], P('ctx', 'head')
- grad_k: bfloat16 [2048, 512], P('ctx', 'head')
- grad_v: bfloat16 [2048, 512], P('ctx', 'head')
All inputs are finite; a program needn't handle non-finite values.
Results may differ from a plain program's by a relative error of at most 0.019.
Values may be sent and summed in bfloat16 or wider, within the bound.
A program may use at most 64 MiB of HBM per device.

v0:
```python
import math

import jax
import jax.numpy as jnp
from jax import lax
from jax.sharding import PartitionSpec as P

HD = 128
GROUP_CH = 16
FEAT = 7
FILT = 128


NEGATIVE = -1e30
EPSILON = 1e-06


def shifted(block, axis, distance):
    devices = range(lax.axis_size(axis))
    route = [(i - distance, i) for i in devices if i - distance in devices]
    return lax.ppermute(block, axis, route)


def earlier_rows(block):
    return shifted(block, "ctx", 1)


def later_rows(block):
    return shifted(block, "ctx", -1)


def channel_total(values):
    return lax.psum(values, "head")


def featurize(extended, taps, count):
    width = taps.shape[0]
    total = jnp.zeros((count, extended.shape[1]), jnp.float32)
    for lag in range(width):
        total = total + taps[lag] * extended[width - 1 - lag : width - 1 - lag + count]
    return total


def featurize_back(extended, taps, count):
    width = taps.shape[0]
    total = jnp.zeros((count, extended.shape[1]), jnp.float32)
    for lag in range(width):
        total = total + taps[lag] * extended[lag : lag + count]
    return total


def band_pair(filter_taps):
    length = filter_taps.shape[0]
    groups = filter_taps.shape[1]
    row_index = lax.broadcasted_iota(jnp.int32, (length, length), 0)
    col_index = lax.broadcasted_iota(jnp.int32, (length, length), 1)
    lag_low = (row_index - col_index).reshape(-1, 1)
    lag_high = lag_low + length
    tap_index = lax.broadcasted_iota(jnp.int32, (length * length, length), 1)
    pick_low = (lag_low == tap_index).astype(jnp.float32)
    pick_high = (lag_high == tap_index).astype(jnp.float32)
    lower = jnp.dot(pick_low, filter_taps, precision=lax.Precision.HIGHEST)
    upper = jnp.dot(pick_high, filter_taps, precision=lax.Precision.HIGHEST)
    lower = jnp.transpose(lower.reshape(length, length, groups), (2, 0, 1))
    upper = jnp.transpose(upper.reshape(length, length, groups), (2, 0, 1))
    return (lower, upper)


def long_filter(extended, lower, upper, count):
    groups, length = (lower.shape[0], lower.shape[1])
    blocks = extended.reshape(count // length + 1, length, groups, GROUP_CH)
    result = jnp.einsum("gtu,bugc->btgc", lower, blocks[1:], precision=lax.Precision.HIGHEST)
    result = result + jnp.einsum(
        "gtu,bugc->btgc", upper, blocks[:-1], precision=lax.Precision.HIGHEST
    )
    return result.reshape(count, groups * GROUP_CH)


def long_filter_back(extended, lower, upper, count):
    groups, length = (lower.shape[0], lower.shape[1])
    blocks = extended.reshape(count // length + 1, length, groups, GROUP_CH)
    result = jnp.einsum("gtu,btgc->bugc", lower, blocks[:-1], precision=lax.Precision.HIGHEST)
    result = result + jnp.einsum(
        "gtu,btgc->bugc", upper, blocks[1:], precision=lax.Precision.HIGHEST
    )
    return result.reshape(count, groups * GROUP_CH)


def block_update(state, query_group, group_pos, key_block, value_block, offset, factor):
    run_max, run_sum, accum = state
    width_block = key_block.shape[0]
    scores = (
        jnp.einsum("thd,phd->htp", query_group, key_block, preferred_element_type=jnp.float32)
        * factor
    )
    key_pos = offset + jnp.arange(width_block, dtype=jnp.int32)
    allowed = (key_pos[None, :] <= group_pos[:, None])[None]
    scores = jnp.where(allowed, scores, NEGATIVE)
    new_max = jnp.maximum(run_max, jnp.max(scores, axis=-1))
    probs = jnp.where(allowed, jnp.exp(scores - new_max[:, :, None]), 0.0)
    rescale = jnp.exp(run_max - new_max)
    new_sum = run_sum * rescale + jnp.sum(probs, axis=-1)
    update = jnp.einsum(
        "htp,phd->htd", probs.astype(jnp.bfloat16), value_block, preferred_element_type=jnp.float32
    )
    return (new_max, new_sum, accum * rescale[:, :, None] + update)


def empty_state(heads, rows):
    return (
        jnp.full((heads, rows), NEGATIVE, jnp.float32),
        jnp.zeros((heads, rows), jnp.float32),
        jnp.zeros((heads, rows, HD), jnp.float32),
    )


def finish_rows(state, channels):
    run_max, run_sum, accum = state
    rows = accum.shape[1]
    return (
        jnp.transpose(accum / run_sum[:, :, None], (1, 0, 2))
        .reshape(rows, channels)
        .astype(jnp.bfloat16)
    )


def per_device(q_att, k_att, v_att, norm_gain, hy_q, hy_k, feat_w, mr_filt, cotangent):
    count, channels = q_att.shape
    heads = channels // HD
    factor = 1.0 / math.sqrt(HD)
    place = lax.axis_index("ctx")
    first = place * count
    groups = ((q_att.reshape(count, heads, HD), first + jnp.arange(count, dtype=jnp.int32)),)
    start_state = tuple((empty_state(heads, group[0].shape[0]) for group in groups))
    carry = start_state
    keys = lax.all_gather(k_att, "ctx", axis=0, tiled=True)
    values = lax.all_gather(v_att, "ctx", axis=0, tiled=True)
    span = keys.shape[0]
    width_block = span
    while width_block > 2048 and width_block % 2 == 0:
        width_block = width_block // 2
    number = span // width_block
    key_blocks = keys.reshape(number, width_block, heads, HD)
    value_blocks = values.reshape(number, width_block, heads, HD)
    offsets = width_block * jnp.arange(number, dtype=jnp.int32)

    def advance(states, inputs):
        key_block, value_block, offset = inputs
        query_group, group_pos = groups[0]
        state = states[0]
        state = block_update(state, query_group, group_pos, key_block, value_block, offset, factor)
        updated = [state]
        return (tuple(updated), None)

    carry, _ = lax.scan(advance, carry, (key_blocks, value_blocks, offsets))
    states = carry
    attended = finish_rows(states[0], channels).astype(jnp.float32)
    width_all = channels * lax.axis_size("head")
    mean_sq = channel_total(jnp.sum(attended * attended, axis=1)) / width_all
    value_stream = (attended * lax.rsqrt(mean_sq + EPSILON)[:, None] * norm_gain).astype(
        jnp.bfloat16
    )
    rim = FEAT - 1
    tail = FILT - 1
    reach = rim + tail
    before = earlier_rows(
        jnp.concatenate(
            [hy_q[count - rim :], hy_k[count - reach :], value_stream[count - reach :]], 0
        )
    )
    q_prev = before[:rim]
    k_prev = before[rim : rim + reach]
    v_prev = before[rim + reach :]
    q_feat = featurize(
        jnp.concatenate([q_prev, hy_q], 0).astype(jnp.float32), feat_w[0], count
    ).astype(jnp.bfloat16)
    k_long = featurize(
        jnp.concatenate([k_prev, hy_k], 0).astype(jnp.float32), feat_w[1], count + tail
    ).astype(jnp.bfloat16)
    v_long = featurize(
        jnp.concatenate([v_prev, value_stream], 0).astype(jnp.float32), feat_w[2], count + tail
    ).astype(jnp.bfloat16)
    mixed_long = (k_long.astype(jnp.float32) * v_long.astype(jnp.float32)).astype(jnp.bfloat16)
    k_feat = k_long[tail:]
    v_feat = v_long[tail:]
    mixed = mixed_long[tail:]
    prior = mixed_long[:tail]
    lower, upper = band_pair(mr_filt)
    zero_row = jnp.zeros((1, channels), jnp.bfloat16)
    signal = long_filter(
        jnp.concatenate([zero_row, prior, mixed], 0).astype(jnp.float32), lower, upper, count
    )
    q_feat32 = q_feat.astype(jnp.float32)
    output = (q_feat32 * signal).astype(jnp.bfloat16)
    grad_out = cotangent.astype(jnp.float32)
    d_signal = (grad_out * q_feat32).astype(jnp.bfloat16)
    d_qf = (grad_out * signal).astype(jnp.bfloat16)
    after = later_rows(d_signal[:tail])
    d_mixed = long_filter_back(
        jnp.concatenate([d_signal, after, zero_row], 0).astype(jnp.float32), lower, upper, count
    )
    d_kf = (d_mixed * v_feat.astype(jnp.float32)).astype(jnp.bfloat16)
    d_vf = (d_mixed * k_feat.astype(jnp.float32)).astype(jnp.bfloat16)
    feature_grads = (d_qf, d_kf, d_vf)
    following = later_rows(jnp.concatenate([grad[:rim] for grad in feature_grads], 0))
    results = []
    for index in range(3):
        extended = jnp.concatenate(
            [feature_grads[index], following[index * rim : (index + 1) * rim]], 0
        ).astype(jnp.float32)
        results.append(featurize_back(extended, feat_w[index], count).astype(jnp.bfloat16))
    return (output, results[0], results[1], results[2])


def solution(mesh):
    placed = (
        P("ctx", "head"),
        P("ctx", "head"),
        P("ctx", "head"),
        P("head"),
        P("ctx", "head"),
        P("ctx", "head"),
        P(None, None, "head"),
        P(None, "head"),
        P("ctx", "head"),
    )
    return jax.shard_map(
        per_device,
        mesh=mesh,
        in_specs=placed,
        out_specs=(P("ctx", "head"), P("ctx", "head"), P("ctx", "head"), P("ctx", "head")),
        check_vma=False,
    )
```

profile of v0, /device:TPU:3, one launch (start us, length us, event | category | flops | bytes accessed | tf_op | source)
XLA Modules:
  0.0 68.2 jit_solution(15300322166727824165)
XLA Ops:
  0.7 10.4 %all_gather.6 = bf16[2048,128]{1,0:T(8,128)(2,1)S(1)} all-gather(bf16[256,128]{1,0:T(8,128)(2,1)} %param.10), channel_id=1, replica_groups=mesh['ctx'=8,'head'=4] {'ctx'}, dimensions={0}, use_global_device_ids=true | all-gather | bytes 589824 | tf_op jit(solution)/shard_map/all_gather | solution.py:136
  11.1 0.6 fusion.84
  11.7 0.6 fusion.5
  12.3 9.2 %all_gather.7 = bf16[2048,128]{1,0:T(8,128)(2,1)S(1)} all-gather(bf16[256,128]{1,0:T(8,128)(2,1)S(1)} %copy-done.4), channel_id=1, replica_groups=mesh['ctx'=8,'head'=4] {'ctx'}, dimensions={0}, use_global_device_ids=true | all-gather | bytes 589824 | tf_op jit(solution)/shard_map/all_gather | solution.py:137
  21.5 0.7 %multiply_reduce_fusion = (f32[256]{0:T(256)S(1)}, f32[256,128]{1,0:T(8,128)S(1)}) fusion(f32[256]{0:T(256)S(1)} %get-tuple-element.66, bf16[2048,128]{1,0:T(8,128)(2,1)S(1)} %all_gather.7, f32[256,2048]{1,0:T(8,128)S(1)} %get-tuple-element.68, f32[256]{0:T(256)S(1)} %broadcast_maximum_fusion, s32[256]{0:T(256)S(1)} %iota_add_fusion, ...), kind=kOutput, calls=%fused_computation.130 | convolution fusion | flops 136511232 | bytes 2757632 | tf_op jit(solution)/shard_map/while/body/eval_jaxpr/htp,phd->htd/dot_general | solution.py:103
  22.2 9.9 %psum.7 = f32[256]{0:T(256)S(1)} all-reduce(f32[256]{0:T(256)S(1)} %get-tuple-element.69), channel_id=1, replica_groups=mesh['ctx'=8,'head'=4] {'head'}, use_global_device_ids=true, to_apply=%region_3.4 | all-reduce | flops 256 | bytes 2048 | tf_op jit(solution)/shard_map/psum | solution.py:33
  32.2 0.1 multiply_convert_fusion.3
  32.4 5.1 %collective-permute-start = (bf16[272,128]{1,0:T(8,128)(2,1)S(1)}, bf16[272,128]{1,0:T(8,128)(2,1)S(1)}, u32[]{:S(2)}, u32[]{:S(2)}) collective-permute-start(bf16[272,128]{1,0:T(8,128)(2,1)S(1)} %pad_maximum_fusion), channel_id=1, source_target_pairs={{0,4},{4,8},{8,12},{12,16},{16,20},{20,24},{24,28},{1,5},{5,9},{9,... | collective-permute-start | bytes 208904 | tf_op jit(solution)/shard_map/ppermute | solution.py:21
  37.6 7.4 %fusion.8 = f32[128,128,8]{1,2,0:T(8,128)S(1)} fusion(f32[128,8]{0,1:T(8,128)S(1)} %copy-done.7, s32[16384]{0:T(1024)S(1)} %subtract_bitcast_fusion), kind=kOutput, calls=%fused_computation.13 | convolution fusion | flops 203423744 | bytes 593920 | tf_op jit(solution)/shard_map/dot_general | solution.py:62
  45.1 7.4 %fusion.7 = f32[128,128,8]{1,2,0:T(8,128)S(1)} fusion(f32[128,8]{0,1:T(8,128)S(1)} %copy-done.7, s32[16384]{0:T(1024)S(1)} %broadcast_add_fusion), kind=kOutput, calls=%fused_computation.12 | convolution fusion | flops 203423744 | bytes 593920 | tf_op jit(solution)/shard_map/dot_general | solution.py:63
  52.6 0.1 pad.12.clone
  52.7 0.1 fusion.43
  52.8 0.1 copy.30
  52.9 1.9 %collective-permute-start.1 = (bf16[127,128]{1,0:T(8,128)(2,1)S(1)}, bf16[127,128]{1,0:T(8,128)(2,1)S(1)}, u32[]{:S(2)}, u32[]{:S(2)}) collective-permute-start(bf16[127,128]{1,0:T(8,128)(2,1)S(1)} %slice.441), channel_id=1, source_target_pairs={{4,0},{8,4},{12,8},{16,12},{20,16},{24,20},{28,24},{5,1},{9,5},{13... | collective-permute-start | bytes 97544 | tf_op jit(solution)/shard_map/ppermute | solution.py:21
  55.0 0.4 multiply_convert_fusion
  55.4 0.1 copy.21
  55.5 0.4 fusion.19
  55.9 0.5 fusion.21
  56.4 0.1 copy.24
  56.6 0.5 fusion.10
  57.2 0.1 copy.28
  57.3 0.7 fusion.42
  58.0 1.1 %collective-permute-done.1 = bf16[127,128]{1,0:T(8,128)(2,1)S(1)} collective-permute-done((bf16[127,128]{1,0:T(8,128)(2,1)S(1)}, bf16[127,128]{1,0:T(8,128)(2,1)S(1)}, u32[]{:S(2)}, u32[]{:S(2)}) %collective-permute-start.1) | collective-permute-done | bytes 32544 | tf_op jit(solution)/shard_map/ppermute | solution.py:21
  59.1 0.1 fusion.72
  59.2 0.1 copy.32
  59.3 0.4 fusion.9
  59.8 0.1 copy.35
  60.0 1.9 %collective-permute-start.2 = (bf16[18,128]{1,0:T(8,128)(2,1)S(1)}, bf16[18,128]{1,0:T(8,128)(2,1)S(1)}, u32[]{:S(2)}, u32[]{:S(2)}) collective-permute-start(bf16[18,128]{1,0:T(8,128)(2,1)S(1)} %pad_maximum_fusion.2), channel_id=1, source_target_pairs={{4,0},{8,4},{12,8},{16,12},{20,16},{24,20},{28,24},{5,1},{9,5},{13... | collective-permute-start | bytes 13832 | tf_op jit(solution)/shard_map/ppermute | solution.py:21
  61.9 3.9 %collective-permute-done.2 = bf16[18,128]{1,0:T(8,128)(2,1)S(1)} collective-permute-done((bf16[18,128]{1,0:T(8,128)(2,1)S(1)}, bf16[18,128]{1,0:T(8,128)(2,1)S(1)}, u32[]{:S(2)}, u32[]{:S(2)}) %collective-permute-start.2) | collective-permute-done | bytes 4640 | tf_op jit(solution)/shard_map/ppermute | solution.py:21
  65.9 0.7 %fusion.45 = bf16[256,128]{1,0:T(8,128)(2,1)} fusion(f32[262,128]{1,0:T(8,128)S(1)} %maximum_convert_fusion.5, f32[128]{0:T(128)S(1)} %get-tuple-element.61, f32[128]{0:T(128)S(1)} %get-tuple-element.60, f32[128]{0:T(128)S(1)} %get-tuple-element.42, f32[128]{0:T(128)S(1)} %get-tuple-element.43, f32[128]{0:T(128)S(1)} %get-tuple-element.44, ...), kind=kLoop, calls=%fused_computation.73 | loop fusion | flops 458752 | bytes 986624 | tf_op jit(solution)/shard_map/convert_element_type | solution.py:211
  66.6 0.7 %fusion.52 = bf16[256,128]{1,0:T(8,128)(2,1)} fusion(f32[262,128]{1,0:T(8,128)S(1)} %maximum_convert_fusion.4, f32[128]{0:T(128)S(1)} %get-tuple-element.47, f32[128]{0:T(128)S(1)} %get-tuple-element.48, f32[128]{0:T(128)S(1)} %get-tuple-element.49, f32[128]{0:T(128)S(1)} %get-tuple-element.50, f32[128]{0:T(128)S(1)} %get-tuple-element.51, ...), kind=kLoop, calls=%fused_computation.87 | loop fusion | flops 458752 | bytes 986624 | tf_op jit(solution)/shard_map/convert_element_type | solution.py:211
  67.4 0.7 %fusion.59 = bf16[256,128]{1,0:T(8,128)(2,1)} fusion(f32[262,128]{1,0:T(8,128)S(1)} %maximum_convert_fusion.3, f32[128]{0:T(128)S(1)} %get-tuple-element.54, f32[128]{0:T(128)S(1)} %get-tuple-element.55, f32[128]{0:T(128)S(1)} %get-tuple-element.56, f32[128]{0:T(128)S(1)} %get-tuple-element.57, f32[128]{0:T(128)S(1)} %get-tuple-element.58, ...), kind=kLoop, calls=%fused_computation.101 | loop fusion | flops 458752 | bytes 986624 | tf_op jit(solution)/shard_map/convert_element_type | solution.py:211
  (53 shorter events, 0.7 us)
Async XLA Ops:
  0.6 10.4 %copy-start = (bf16[256,128]{1,0:T(8,128)(2,1)S(1)}, bf16[256,128]{1,0:T(8,128)(2,1)}, u32[]{:S(2)}) copy-start(bf16[256,128]{1,0:T(8,128)(2,1)} %param.9) | copy-start | bytes 196612
  11.0 1.2 %copy-start.4 = (bf16[256,128]{1,0:T(8,128)(2,1)S(1)}, bf16[256,128]{1,0:T(8,128)(2,1)}, u32[]{:S(2)}) copy-start(bf16[256,128]{1,0:T(8,128)(2,1)} %param.11) | copy-start | bytes 196612
  21.5 10.7 %copy-start.6 = (f32[128]{0:T(128)S(1)}, f32[128]{0:T(128)}, u32[]{:S(2)}) copy-start(f32[128]{0:T(128)} %param.12) | copy-start | bytes 1540
  21.5 10.8 %copy-start.2 = (bf16[256,128]{1,0:T(8,128)(2,1)S(1)}, bf16[256,128]{1,0:T(8,128)(2,1)}, u32[]{:S(2)}) copy-start(bf16[256,128]{1,0:T(8,128)(2,1)} %param.14) | copy-start | bytes 196612
  21.5 10.9 %copy-start.3 = (bf16[256,128]{1,0:T(8,128)(2,1)S(1)}, bf16[256,128]{1,0:T(8,128)(2,1)}, u32[]{:S(2)}) copy-start(bf16[256,128]{1,0:T(8,128)(2,1)} %param.13) | copy-start | bytes 196612
  21.5 16.1 %copy-start.5 = (f32[3,7,128]{2,1,0:T(8,128)S(1)}, f32[3,7,128]{2,1,0:T(8,128)}, u32[]{:S(2)}) copy-start(f32[3,7,128]{2,1,0:T(8,128)} %param.15) | copy-start | bytes 32260
  21.5 16.1 %copy-start.7 = (f32[128,8]{0,1:T(8,128)S(1)}, f32[128,8]{0,1:T(8,128)}, u32[]{:S(2)}) copy-start(f32[128,8]{0,1:T(8,128)} %param.16) | copy-start | bytes 12292
  32.4 20.3 %collective-permute-start = (bf16[272,128]{1,0:T(8,128)(2,1)S(1)}, bf16[272,128]{1,0:T(8,128)(2,1)S(1)}, u32[]{:S(2)}, u32[]{:S(2)}) collective-permute-start(bf16[272,128]{1,0:T(8,128)(2,1)S(1)} %pad_maximum_fusion), channel_id=1, source_target_pairs={{0,4},{4,8},{8,12},{12,16},{16,20},{20,24},{24,28},{1,5},{5,9},{9,... | collective-permute-start | bytes 208904 | tf_op jit(solution)/shard_map/ppermute | solution.py:21
  37.6 15.0 %copy-start.1 = (bf16[256,128]{1,0:T(8,128)(2,1)S(1)}, bf16[256,128]{1,0:T(8,128)(2,1)}, u32[]{:S(2)}) copy-start(bf16[256,128]{1,0:T(8,128)(2,1)} %param.17) | copy-start | bytes 196612
  52.9 6.1 %collective-permute-start.1 = (bf16[127,128]{1,0:T(8,128)(2,1)S(1)}, bf16[127,128]{1,0:T(8,128)(2,1)S(1)}, u32[]{:S(2)}, u32[]{:S(2)}) collective-permute-start(bf16[127,128]{1,0:T(8,128)(2,1)S(1)} %slice.441), channel_id=1, source_target_pairs={{4,0},{8,4},{12,8},{16,12},{20,16},{24,20},{28,24},{5,1},{9,5},{13... | collective-permute-start | bytes 97544 | tf_op jit(solution)/shard_map/ppermute | solution.py:21
  60.0 5.8 %collective-permute-start.2 = (bf16[18,128]{1,0:T(8,128)(2,1)S(1)}, bf16[18,128]{1,0:T(8,128)(2,1)S(1)}, u32[]{:S(2)}, u32[]{:S(2)}) collective-permute-start(bf16[18,128]{1,0:T(8,128)(2,1)S(1)} %pad_maximum_fusion.2), channel_id=1, source_target_pairs={{4,0},{8,4},{12,8},{16,12},{20,16},{24,20},{28,24},{5,1},{9,5},{13... | collective-permute-start | bytes 13832 | tf_op jit(solution)/shard_map/ppermute | solution.py:21
where the time goes:
time: 68.5 us; the launch traced here: 68.2 us
  blocking collectives  29.5 us (43%)
  matrix products  18.1 us (26%)
  starting transfers between devices  8.99 us (13%)
  waiting for transfers between devices  5.01 us (7%)
  other arithmetic  4.45 us (6%)
  local copies, waits for them, and re-layouts  1.12 us (2%)
  between operations  1.04 us (2%)
    all_gather x1, blocking collectives, per_device(): keys = lax.all_gather(k_att, 'ctx', axis=0, tiled=True)  10.4 us
    psum x1, blocking collectives, channel_total(): return lax.psum(values, 'head')  9.95 us
    all_gather x1, blocking collectives, per_device(): values = lax.all_gather(v_att, 'ctx', axis=0, tiled=True)  9.17 us
    ppermute x3, starting transfers between devices, shifted(): return lax.ppermute(block, axis, route)  8.99 us
    dot_general x1, matrix products, band_pair(): lower = jnp.dot(pick_low, filter_taps, precision=lax.Precision.HIGHEST)  7.45 us
    dot_general x1, matrix products, band_pair(): upper = jnp.dot(pick_high, filter_taps, precision=lax.Precision.HIGHEST)  7.45 us
    ppermute x3, waiting for transfers between devices, shifted(): return lax.ppermute(block, axis, route)  5.01 us
    convert_element_type x3, other arithmetic, per_device(): featurize_back(extended, feat_w[index], count).astype(jnp.bfloat16)  2.24 us
  transfers between devices with their start and end apart: 3, of which 2 were waited for; matrix products, arithmetic and copies ran while one was open for 26% of the time, Pallas kernels for 0%

commit v1 on v0

v1 whole, which is shorter than its diff:
```python
import functools
import math

import jax
import jax.numpy as jnp
from jax import lax
from jax.experimental import pallas as pl
from jax.experimental.pallas import tpu as pltpu
from jax.sharding import PartitionSpec as P

HD = 128
GROUP_CH = 16
FEAT = 7
FILT = 128
NEGATIVE = -1e30
EPSILON = 1e-06
FAR = 144
NEAR = 16
MESH = pl.DeviceIdType.MESH
F32 = jnp.float32
BF16 = jnp.bfloat16


def taps_sum(ref, start, count, weights, step):
    total = weights[0:1] * ref[pl.ds(start, count), :]
    for lag in range(1, FEAT):
        total = total + weights[lag : lag + 1] * ref[pl.ds(start + step * lag, count), :]
    return total


def band_product(taps_ref, window_ref, groups, lane_group):
    wide = jnp.concatenate([window_ref[0:256, :], window_ref[128:384, :]], 1)
    short = jnp.concatenate([taps_ref[g * FILT : g * FILT + NEAR, :] for g in range(groups)], 0)
    last = jnp.dot(short, window_ref[256:512, :], preferred_element_type=F32)
    first = second = third = None
    for g in range(groups):
        both = jnp.dot(taps_ref[g * FILT : (g + 1) * FILT, :], wide, preferred_element_type=F32)
        end = last[g * NEAR : (g + 1) * NEAR]
        if g == 0:
            first, second, third = both[:, :128], both[:, 128:], end
        else:
            mine = lane_group == g
            first = jnp.where(mine, both[:, :128], first)
            second = jnp.where(mine, both[:, 128:], second)
            third = jnp.where(mine, end, third)
    return jnp.concatenate([first, second, third], 0)


def kernel(
    n,
    heads,
    width,
    q_ref,
    k_ref,
    v_ref,
    gain_ref,
    hyq_ref,
    hyk_ref,
    fw_ref,
    mr_ref,
    cot_ref,
    out_ref,
    gq_ref,
    gk_ref,
    gv_ref,
    kv,
    q_ext,
    aft_kv,
    hyk_ext,
    hyq_ext,
    cot_ext,
    squares,
    taps_f,
    taps_b,
    win_f,
    win_b,
    m_ref,
    l_ref,
    acc_ref,
    x32,
    y32,
    dq32,
    dk32,
    dv32,
    halo_send,
    halo_recv,
    kv_send,
    fwd_send,
    kv_recv,
    sib_send,
    sq_send,
    sq_recv,
):
    count = q_ref.shape[0]
    groups = mr_ref.shape[1]
    rows = FAR + count + NEAR
    chips = n // 2
    me = lax.axis_index("ctx")
    head = lax.axis_index("head")
    chip = me // 2
    core = lax.rem(me, 2)
    sibling = me + 1 - 2 * core

    barrier = pltpu.get_barrier_semaphore()

    def greet_ctx(d, c):
        pl.semaphore_signal(
            barrier, inc=1, device_id={"ctx": lax.rem(me + d, n)}, device_id_type=MESH
        )
        return c

    lax.fori_loop(1, n, greet_ctx, 0)
    for d in range(1, heads):
        pl.semaphore_signal(
            barrier, inc=1, device_id={"head": lax.rem(head + d, heads)}, device_id_type=MESH
        )
    kv[me, 0] = k_ref[...]
    kv[me, 1] = v_ref[...]
    q_ext[FAR : FAR + count, :] = q_ref[...]
    hyk_ext[FAR : FAR + count, :] = hyk_ref[...]
    hyq_ext[NEAR : NEAR + count, :] = hyq_ref[...]
    cot_ext[0:count, :] = cot_ref[...]

    def halo(index, src, dst, target):
        return pltpu.make_async_remote_copy(
            src_ref=src,
            dst_ref=dst,
            send_sem=halo_send.at[index],
            recv_sem=halo_recv.at[index],
            device_id={"ctx": target},
            device_id_type=MESH,
        )

    up = jnp.minimum(me + 1, n - 1)
    down = jnp.maximum(me - 1, 0)
    tail = pl.ds(count - FAR, FAR)
    onward = [
        halo(0, q_ref.at[tail, :], q_ext.at[pl.ds(0, FAR), :], up),
        halo(1, hyk_ref.at[tail, :], hyk_ext.at[pl.ds(0, FAR), :], up),
        halo(2, hyq_ref.at[pl.ds(count - NEAR, NEAR), :], hyq_ext.at[pl.ds(0, NEAR), :], up),
    ]
    near = pl.ds(0, NEAR)
    far = pl.ds(0, FAR)
    back = [
        halo(3, hyq_ref.at[far, :], hyq_ext.at[pl.ds(NEAR + count, FAR), :], down),
        halo(4, cot_ref.at[far, :], cot_ext.at[pl.ds(count, FAR), :], down),
        halo(5, q_ref.at[near, :], q_ext.at[pl.ds(FAR + count, NEAR), :], down),
        halo(6, hyk_ref.at[near, :], hyk_ext.at[pl.ds(FAR + count, NEAR), :], down),
        halo(7, k_ref.at[near, :], aft_kv.at[0], down),
        halo(8, v_ref.at[near, :], aft_kv.at[1], down),
    ]

    def kv_copy(slot, target, sem):
        return pltpu.make_async_remote_copy(
            src_ref=kv.at[slot],
            dst_ref=kv.at[slot],
            send_sem=sem,
            recv_sem=kv_recv.at[slot],
            device_id={"ctx": target},
            device_id_type=MESH,
        )

    pl.semaphore_wait(barrier, n + heads - 2)

    @pl.when(me < n - 1)
    def _():
        for copy in onward:
            copy.start()

    @pl.when(me > 0)
    def _():
        for copy in back:
            copy.start()

    def send_own(d, c):
        kv_copy(me, me + 2 * d, kv_send.at[d]).start()
        return c

    lax.fori_loop(1, chips - chip, send_own, 0)

    @pl.when(core == 0)
    def _():
        kv_copy(me, sibling, sib_send).start()

    @pl.when(me == 0)
    def _():
        q_ext[0:FAR, :] = jnp.zeros((FAR, HD), BF16)
        hyk_ext[0:FAR, :] = jnp.zeros((FAR, HD), BF16)
        hyq_ext[0:NEAR, :] = jnp.zeros((NEAR, HD), BF16)

    @pl.when(me == n - 1)
    def _():
        hyq_ext[NEAR + count : NEAR + count + FAR, :] = jnp.zeros((FAR, HD), BF16)
        cot_ext[count : count + FAR, :] = jnp.zeros((FAR, HD), BF16)
        q_ext[FAR + count :, :] = jnp.zeros((NEAR, HD), BF16)
        hyk_ext[FAR + count :, :] = jnp.zeros((NEAR, HD), BF16)
        aft_kv[...] = jnp.zeros(aft_kv.shape, BF16)

    tap = lax.broadcasted_iota(jnp.int32, (FILT, 2 * FILT), 0)
    col = lax.broadcasted_iota(jnp.int32, (FILT, 2 * FILT), 1)
    taps16 = mr_ref[...].astype(BF16)
    over_rows = (((0,), (0,)), ((), ()))
    for out_taps, place in ((taps_b, tap == col), (taps_f, tap == FILT - col)):
        line = lax.dot_general(
            taps16, place.astype(F32).astype(BF16), over_rows, preferred_element_type=F32
        )
        for g in range(groups):
            spread = jnp.broadcast_to(line[g : g + 1, :], (FILT, 2 * FILT))
            moved = pltpu.roll(spread, 0, 1, stride=1, stride_axis=0)
            out_taps[g * FILT : (g + 1) * FILT, :] = moved.astype(BF16)

    scale = math.log2(math.e) / math.sqrt(HD)
    over_last = (((1,), (1,)), ((), ()))

    def attend(start, size, keys, values, key_base, masked):
        part = pl.ds(start, size)
        scores = lax.dot_general(q_ext[part, :], keys, over_last, preferred_element_type=F32)
        if masked:
            row = lax.broadcasted_iota(jnp.int32, scores.shape, 0) + (start - FAR)
            at = lax.broadcasted_iota(jnp.int32, scores.shape, 1) + key_base
            scores = jnp.where(at <= row, scores, NEGATIVE)
        old = m_ref[part, :]
        new = jnp.maximum(old, jnp.max(scores, axis=1, keepdims=True))
        m_ref[part, :] = new
        factor = jnp.exp2((old - new) * scale)
        probs = jnp.exp2((scores - new[:, 0:1]) * scale)
        if probs.shape[1] == 2 * HD:
            sums = probs[:, :HD] + probs[:, HD:]
        else:
            lane0 = lax.broadcasted_iota(jnp.int32, (size, HD), 1) == 0
            sums = jnp.where(lane0, jnp.sum(probs, axis=1, keepdims=True), 0.0)
        l_ref[part, :] = l_ref[part, :] * factor + sums
        acc_ref[part, :] = acc_ref[part, :] * factor + jnp.dot(
            probs.astype(BF16), values, preferred_element_type=F32
        )

    m_ref[...] = jnp.full(m_ref.shape, NEGATIVE, F32)
    l_ref[...] = jnp.zeros(l_ref.shape, F32)
    acc_ref[...] = jnp.zeros(acc_ref.shape, F32)

    @pl.when(me > 0)
    def _():
        for copy in onward:
            copy.wait_recv()

    @pl.when(me < n - 1)
    def _():
        for copy in back:
            copy.wait_recv()

    attend(0, rows, kv[me, 0], kv[me, 1], 0, True)
    attend(FAR + count, NEAR, aft_kv[0], aft_kv[1], count, True)

    lane_group = lax.broadcasted_iota(jnp.int32, (1, HD), 1) // GROUP_CH
    ext = 384 + NEAR
    x32[...] = hyq_ext[...].astype(F32)
    qf = taps_sum(x32, NEAR, ext, fw_ref[0], -1).astype(BF16).astype(F32)
    d_signal = (cot_ext[...].astype(F32) * qf).astype(BF16)
    win_b[0:ext, :] = d_signal
    win_b[ext:, :] = jnp.zeros((512 - ext, HD), BF16)
    win_f[ext:, :] = jnp.zeros((512 - ext, HD), BF16)
    y32[...] = hyk_ext[...].astype(F32)
    kf = taps_sum(y32, NEAR, ext, fw_ref[1], -1).astype(BF16).astype(F32)
    near_rows = count + NEAR
    d_mixed = band_product(taps_b, win_b, groups, lane_group)
    dv32[...] = (d_mixed * kf[FILT : FILT + near_rows]).astype(BF16).astype(F32)
    gv_ref[...] = taps_sum(dv32, 0, count, fw_ref[2], 1).astype(BF16)
    dk32[...] = d_mixed

    @pl.when(core == 1)
    def _():
        kv_copy(sibling, sibling, sib_send).wait_recv()
        attend(0, rows, kv[sibling, 0], kv[sibling, 1], -count, True)

    def remote(d, c):
        same = me - 2 * d
        other = sibling - 2 * d
        kv_copy(same, sibling, fwd_send.at[d]).wait_recv()
        kv_copy(same, sibling, fwd_send.at[d]).start()
        attend(0, rows, kv[same, 0], kv[same, 1], (same - me) * count, True)
        kv_copy(other, sibling, fwd_send.at[d]).wait_recv()
        attend(0, rows, kv[other, 0], kv[other, 1], (other - me) * count, True)
        return c

    lax.fori_loop(1, chip + 1, remote, 0)

    total = jnp.sum(l_ref[...], axis=1, keepdims=True)
    attended = (acc_ref[...] / total).astype(BF16).astype(F32)
    squares[head] = jnp.zeros((8, 512), F32)
    squares[head, :, 0:rows] = lax.dot_general(
        jnp.ones((8, HD), F32),
        attended * attended,
        over_last,
        precision=lax.Precision.HIGHEST,
        preferred_element_type=F32,
    )

    def sq_copy(d):
        return pltpu.make_async_remote_copy(
            src_ref=squares.at[head],
            dst_ref=squares.at[head],
            send_sem=sq_send.at[d],
            recv_sem=sq_recv.at[d],
            device_id={"head": lax.rem(head + d, heads)},
            device_id_type=MESH,
        )

    for d in range(1, heads):
        sq_copy(d).start()
    for d in range(1, heads):
        sq_copy(d).wait_recv()
    whole = squares[0]
    for other in range(1, heads):
        whole = whole + squares[other]
    mean_sq = lax.dot_general(
        whole,
        jnp.full((8, HD), 1.0 / (8 * width), F32),
        over_rows,
        precision=lax.Precision.HIGHEST,
        preferred_element_type=F32,
    )[0:rows]
    value = (attended * lax.rsqrt(mean_sq + EPSILON) * gain_ref[...]).astype(BF16).astype(F32)
    place = lax.broadcasted_iota(jnp.int32, value.shape, 0) + (me * count - FAR)
    x32[...] = jnp.where((place >= 0) & (place < n * count), value, 0.0)
    vf = taps_sum(x32, NEAR, ext, fw_ref[2], -1).astype(BF16).astype(F32)
    win_f[0:ext, :] = (kf * vf).astype(BF16)
    signal = band_product(taps_f, win_f, groups, lane_group)
    out_ref[...] = (qf[0:count] * signal[0:count]).astype(BF16)
    dq32[...] = (cot_ext[0:near_rows, :].astype(F32) * signal).astype(BF16).astype(F32)
    gq_ref[...] = taps_sum(dq32, 0, count, fw_ref[0], 1).astype(BF16)
    dk32[...] = (dk32[...] * vf[FILT : FILT + near_rows]).astype(BF16).astype(F32)
    gk_ref[...] = taps_sum(dk32, 0, count, fw_ref[1], 1).astype(BF16)

    @pl.when(me < n - 1)
    def _():
        for copy in onward:
            copy.wait_send()

    @pl.when(me > 0)
    def _():
        for copy in back:
            copy.wait_send()

    @pl.when(core == 0)
    def _():
        kv_copy(me, sibling, sib_send).wait_send()

    def sent_own(d, c):
        kv_copy(me, me + 2 * d, kv_send.at[d]).wait_send()
        return c

    lax.fori_loop(1, chips - chip, sent_own, 0)

    def sent_on(d, c):
        kv_copy(me - 2 * d, sibling, fwd_send.at[d]).wait_send()
        return c

    lax.fori_loop(1, chip + 1, sent_on, 0)
    for d in range(1, heads):
        sq_copy(d).wait_send()


def per_device(q_att, k_att, v_att, norm_gain, hy_q, hy_k, feat_w, mr_filt, cotangent):
    count, channels = q_att.shape
    n = lax.axis_size("ctx")
    heads = lax.axis_size("head")
    groups = mr_filt.shape[1]
    rows = FAR + count + NEAR
    block = jax.ShapeDtypeStruct((count, channels), BF16)
    vmem = pl.BlockSpec(memory_space=pltpu.VMEM)
    dma = pltpu.SemaphoreType.DMA
    near_rows = count + NEAR
    return pl.pallas_call(
        functools.partial(kernel, n, heads, channels * heads),
        out_shape=(block,) * 4,
        in_specs=[vmem] * 9,
        out_specs=(vmem,) * 4,
        scratch_shapes=[
            pltpu.VMEM((n, 2, count, HD), BF16),
            pltpu.VMEM((rows, HD), BF16),
            pltpu.VMEM((2, NEAR, HD), BF16),
            pltpu.VMEM((rows, HD), BF16),
            pltpu.VMEM((rows, HD), BF16),
            pltpu.VMEM((count + FAR, HD), BF16),
            pltpu.VMEM((heads, 8, 512), F32),
            pltpu.VMEM((groups * FILT, 2 * FILT), BF16),
            pltpu.VMEM((groups * FILT, 2 * FILT), BF16),
            pltpu.VMEM((512, HD), BF16),
            pltpu.VMEM((512, HD), BF16),
            pltpu.VMEM((rows, HD), F32),
            pltpu.VMEM((rows, HD), F32),
            pltpu.VMEM((rows, HD), F32),
            pltpu.VMEM((rows, HD), F32),
            pltpu.VMEM((rows, HD), F32),
            pltpu.VMEM((near_rows, HD), F32),
            pltpu.VMEM((near_rows, HD), F32),
            pltpu.VMEM((near_rows, HD), F32),
            dma((9,)),
            dma((9,)),
            dma((n // 2,)),
            dma((n // 2,)),
            dma((n,)),
            dma,
            dma((heads,)),
            dma((heads,)),
        ],
        compiler_params=pltpu.CompilerParams(
            collective_id=0, has_side_effects=True, vmem_limit_bytes=40 * 1024 * 1024
        ),
    )(q_att, k_att, v_att, norm_gain.reshape(1, channels), hy_q, hy_k, feat_w, mr_filt, cotangent)


def solution(mesh):
    placed = (
        P("ctx", "head"),
        P("ctx", "head"),
        P("ctx", "head"),
        P("head"),
        P("ctx", "head"),
        P("ctx", "head"),
        P(None, None, "head"),
        P(None, "head"),
        P("ctx", "head"),
    )
    return jax.shard_map(
        per_device,
        mesh=mesh,
        in_specs=placed,
        out_specs=(P("ctx", "head"),) * 4,
        check_vma=False,
    )
```

time: 68.5 us -> 30 us (0.44)
  the two profiles are of different devices: /device:TPU:3 before, /device:TPU:6 now
where the time goes in v1:
time: 30 us; the launch traced here: 29.4 us
  Pallas kernels  20.5 us (68%)
  local copies, waits for them, and re-layouts  8.24 us (27%)
  between operations  0.68 us (2%)
    pallas_call x1, Pallas kernels, per_device(): pl.pallas_call(functools.partial(kernel, n, heads, channels * heads), out...  20.5 us
    unnamed x21, local copies, waits for them, and re-layouts  8.24 us

profile of v1, /device:TPU:6, one launch (start us, length us, event | category | flops | bytes accessed | tf_op | source)
XLA Modules:
  0.0 29.4 jit_solution(3916700254951719447)
XLA Ops:
  0.6 0.0 copy-start
  0.6 0.0 copy-start.7
  0.7 0.8 %copy.13.mr_ref = f32[128,8]{1,0:T(8,128)S(1)} copy(f32[128,8]{0,1:T(8,128)} %param.16) | data formatting | bytes 8192 | tf_op args[7]
  1.5 0.0 copy-done
  1.5 0.0 copy-done.7
  1.5 0.0 copy-start.1
  1.5 0.8 %copy-done.1 = bf16[256,128]{1,0:T(8,128)(2,1)S(1)} copy-done((bf16[256,128]{1,0:T(8,128)(2,1)S(1)}, bf16[256,128]{1,0:T(8,128)(2,1)}, u32[]{:S(2)}) %copy-start.1) | copy-done | bytes 65560
  2.3 0.0 copy-start.2
  2.3 0.8 %copy-done.2 = bf16[256,128]{1,0:T(8,128)(2,1)S(1)} copy-done((bf16[256,128]{1,0:T(8,128)(2,1)S(1)}, bf16[256,128]{1,0:T(8,128)(2,1)}, u32[]{:S(2)}) %copy-start.2) | copy-done | bytes 65560
  3.2 0.0 copy-start.3
  3.2 0.8 %copy-done.3 = bf16[256,128]{1,0:T(8,128)(2,1)S(1)} copy-done((bf16[256,128]{1,0:T(8,128)(2,1)S(1)}, bf16[256,128]{1,0:T(8,128)(2,1)}, u32[]{:S(2)}) %copy-start.3) | copy-done | bytes 65560
  4.0 0.0 copy-start.4
  4.0 0.8 %copy-done.4 = bf16[256,128]{1,0:T(8,128)(2,1)S(1)} copy-done((bf16[256,128]{1,0:T(8,128)(2,1)S(1)}, bf16[256,128]{1,0:T(8,128)(2,1)}, u32[]{:S(2)}) %copy-start.4) | copy-done | bytes 65560
  4.8 0.0 copy-start.5
  4.8 0.8 %copy-done.5 = bf16[256,128]{1,0:T(8,128)(2,1)S(1)} copy-done((bf16[256,128]{1,0:T(8,128)(2,1)S(1)}, bf16[256,128]{1,0:T(8,128)(2,1)}, u32[]{:S(2)}) %copy-start.5) | copy-done | bytes 65560
  5.7 0.0 copy-start.6
  5.7 0.7 %copy-done.6 = f32[3,7,128]{2,1,0:T(8,128)S(1)} copy-done((f32[3,7,128]{2,1,0:T(8,128)S(1)}, f32[3,7,128]{2,1,0:T(8,128)}, u32[]{:S(2)}) %copy-start.6) | copy-done | bytes 10776
  6.4 20.5 %shard_map.120 = (bf16[256,128]{1,0:T(8,128)(2,1)S(1)}, bf16[256,128]{1,0:T(8,128)(2,1)S(1)}, bf16[256,128]{1,0:T(8,128)(2,1)S(1)}, bf16[256,128]{1,0:T(8,128)(2,1)S(1)}) custom-call(bf16[256,128]{1,0:T(8,128)(2,1)S(1)} %copy-done, bf16[256,128]{1,0:T(8,128)(2,1)S(1)} %copy-done.1, bf16[256,128]{1,0:T(8,128)(2,1)S(1)} %copy-done.2, f32[1,128]{1,0:T(1,128)S(1)} %bitcast.1, ...), custom_call_target="tpu_custom_call" | custom-call | tf_op jit(solution)/shard_map/pallas_call | solution.py:373
  26.9 0.6 %copy.18 = bf16[256,128]{1,0:T(8,128)(2,1)} copy(bf16[256,128]{1,0:T(8,128)(2,1)S(1)} %get-tuple-element.8) | data formatting | bytes 131072
  27.5 0.6 %copy.19 = bf16[256,128]{1,0:T(8,128)(2,1)} copy(bf16[256,128]{1,0:T(8,128)(2,1)S(1)} %get-tuple-element.9) | data formatting | bytes 131072
  28.2 0.6 %copy.20 = bf16[256,128]{1,0:T(8,128)(2,1)} copy(bf16[256,128]{1,0:T(8,128)(2,1)S(1)} %get-tuple-element.10) | data formatting | bytes 131072
  28.8 0.6 %copy.21 = bf16[256,128]{1,0:T(8,128)(2,1)} copy(bf16[256,128]{1,0:T(8,128)(2,1)S(1)} %get-tuple-element.11) | data formatting | bytes 131072
Async XLA Ops:
  0.6 0.8 %copy-start = (bf16[256,128]{1,0:T(8,128)(2,1)S(1)}, bf16[256,128]{1,0:T(8,128)(2,1)}, u32[]{:S(2)}) copy-start(bf16[256,128]{1,0:T(8,128)(2,1)} %q_ref.1) | copy-start | bytes 196612
  0.6 0.8 %copy-start.7 = (f32[128]{0:T(128)S(1)}, f32[128]{0:T(128)}, u32[]{:S(2)}) copy-start(f32[128]{0:T(128)} %param.12) | copy-start | bytes 1540
  1.5 0.8 %copy-start.1 = (bf16[256,128]{1,0:T(8,128)(2,1)S(1)}, bf16[256,128]{1,0:T(8,128)(2,1)}, u32[]{:S(2)}) copy-start(bf16[256,128]{1,0:T(8,128)(2,1)} %k_ref.1) | copy-start | bytes 196612
  2.3 0.8 %copy-start.2 = (bf16[256,128]{1,0:T(8,128)(2,1)S(1)}, bf16[256,128]{1,0:T(8,128)(2,1)}, u32[]{:S(2)}) copy-start(bf16[256,128]{1,0:T(8,128)(2,1)} %v_ref.1) | copy-start | bytes 196612
  3.2 0.8 %copy-start.3 = (bf16[256,128]{1,0:T(8,128)(2,1)S(1)}, bf16[256,128]{1,0:T(8,128)(2,1)}, u32[]{:S(2)}) copy-start(bf16[256,128]{1,0:T(8,128)(2,1)} %hyq_ref.1) | copy-start | bytes 196612
  4.0 0.8 %copy-start.4 = (bf16[256,128]{1,0:T(8,128)(2,1)S(1)}, bf16[256,128]{1,0:T(8,128)(2,1)}, u32[]{:S(2)}) copy-start(bf16[256,128]{1,0:T(8,128)(2,1)} %hyk_ref.1) | copy-start | bytes 196612
  4.8 0.8 %copy-start.5 = (bf16[256,128]{1,0:T(8,128)(2,1)S(1)}, bf16[256,128]{1,0:T(8,128)(2,1)}, u32[]{:S(2)}) copy-start(bf16[256,128]{1,0:T(8,128)(2,1)} %cot_ref.1) | copy-start | bytes 196612
  5.7 0.7 %copy-start.6 = (f32[3,7,128]{2,1,0:T(8,128)S(1)}, f32[3,7,128]{2,1,0:T(8,128)}, u32[]{:S(2)}) copy-start(f32[3,7,128]{2,1,0:T(8,128)} %fw_ref.1) | copy-start | bytes 32260

commit v2 on v1

--- a/solution.py
+++ b/solution.py
@@ -53,16 +53,13 @@
     q_ref,
     k_ref,
     v_ref,
-    gain_ref,
+    gain_hbm,
     hyq_ref,
     hyk_ref,
-    fw_ref,
-    mr_ref,
+    fw_hbm,
+    mr_hbm,
     cot_ref,
-    out_ref,
-    gq_ref,
-    gk_ref,
-    gv_ref,
+    packed_ref,
     kv,
     q_ext,
     aft_kv,
@@ -82,17 +79,24 @@
     dq32,
     dk32,
     dv32,
+    gain_ref,
+    fw_ref,
+    mr_ref,
+    stage,
+    local_sem,
+    out_sem,
     halo_send,
     halo_recv,
     kv_send,
     fwd_send,
+    relay_send,
     kv_recv,
     sib_send,
     sq_send,
     sq_recv,
 ):
     count = q_ref.shape[0]
-    groups = mr_ref.shape[1]
+    groups = mr_ref.shape[0]
     rows = FAR + count + NEAR
     chips = n // 2
     me = lax.axis_index("ctx")
@@ -101,6 +105,24 @@
     core = lax.rem(me, 2)
     sibling = me + 1 - 2 * core
 
+    moves = (
+        (k_ref, kv.at[0, me]),
+        (v_ref, kv.at[1, me]),
+        (mr_hbm, mr_ref),
+        (q_ref, q_ext.at[pl.ds(FAR, count), :]),
+        (hyq_ref, hyq_ext.at[pl.ds(NEAR, count), :]),
+        (cot_ref, cot_ext.at[pl.ds(0, count), :]),
+        (fw_hbm, fw_ref),
+        (hyk_ref, hyk_ext.at[pl.ds(FAR, count), :]),
+        (gain_hbm, gain_ref),
+    )
+    loads = [
+        pltpu.make_async_copy(src, dst, local_sem.at[index])
+        for index, (src, dst) in enumerate(moves)
+    ]
+    for load in loads:
+        load.start()
+
     barrier = pltpu.get_barrier_semaphore()
 
     def greet_ctx(d, c):
@@ -114,12 +136,6 @@
         pl.semaphore_signal(
             barrier, inc=1, device_id={"head": lax.rem(head + d, heads)}, device_id_type=MESH
         )
-    kv[me, 0] = k_ref[...]
-    kv[me, 1] = v_ref[...]
-    q_ext[FAR : FAR + count, :] = q_ref[...]
-    hyk_ext[FAR : FAR + count, :] = hyk_ref[...]
-    hyq_ext[NEAR : NEAR + count, :] = hyq_ref[...]
-    cot_ext[0:count, :] = cot_ref[...]
 
     def halo(index, src, dst, target):
         return pltpu.make_async_remote_copy(
@@ -150,17 +166,56 @@
         halo(8, v_ref.at[near, :], aft_kv.at[1], down),
     ]
 
-    def kv_copy(slot, target, sem):
+    def kv_copy(half, slot, target, sem):
         return pltpu.make_async_remote_copy(
-            src_ref=kv.at[slot],
-            dst_ref=kv.at[slot],
+            src_ref=kv.at[half, slot],
+            dst_ref=kv.at[half, slot],
             send_sem=sem,
-            recv_sem=kv_recv.at[slot],
+            recv_sem=kv_recv.at[half, slot],
             device_id={"ctx": target},
             device_id_type=MESH,
         )
 
+    square = chips == 4
+
+    def each_own(act):
+        def one(d, c):
+            for half in range(2):
+                act(kv_copy(half, me, me + 2 * d, kv_send.at[half, d]))
+            return c
+
+        if square:
+
+            @pl.when(chip != 1)
+            def _():
+                lax.fori_loop(1, jnp.minimum(chips - chip, 3), one, 0)
+
+            @pl.when(chip == 1)
+            def _():
+                one(2, 0)
+        else:
+            lax.fori_loop(1, chips - chip, one, 0)
+
+    def each_relay(half, earlier, act):
+        if not square:
+            return
+
+        @pl.when((chip == 1 + half) & (earlier == 0))
+        def _():
+            act(kv_copy(half, core, 6 + core, relay_send.at[half]))
+
+        @pl.when((chip == 3) & (earlier == 1))
+        def _():
+            act(kv_copy(half, 2 + core, 4 + core, relay_send.at[half]))
+
+    def source(step):
+        if square:
+            return lax.rem(step + jnp.where(chip == 3, 1, 0), jnp.maximum(chip, 1))
+        return chip - 1 - step
+
     pl.semaphore_wait(barrier, n + heads - 2)
+    loads[0].wait()
+    loads[1].wait()
 
     @pl.when(me < n - 1)
     def _():
@@ -172,15 +227,12 @@
         for copy in back:
             copy.start()
 
-    def send_own(d, c):
-        kv_copy(me, me + 2 * d, kv_send.at[d]).start()
-        return c
-
-    lax.fori_loop(1, chips - chip, send_own, 0)
+    each_own(lambda copy: copy.start())
 
     @pl.when(core == 0)
     def _():
-        kv_copy(me, sibling, sib_send).start()
+        for half in range(2):
+            kv_copy(half, me, sibling, sib_send.at[half]).start()
 
     @pl.when(me == 0)
     def _():
@@ -196,14 +248,13 @@
         hyk_ext[FAR + count :, :] = jnp.zeros((NEAR, HD), BF16)
         aft_kv[...] = jnp.zeros(aft_kv.shape, BF16)
 
+    loads[2].wait()
+
     tap = lax.broadcasted_iota(jnp.int32, (FILT, 2 * FILT), 0)
     col = lax.broadcasted_iota(jnp.int32, (FILT, 2 * FILT), 1)
     taps16 = mr_ref[...].astype(BF16)
-    over_rows = (((0,), (0,)), ((), ()))
     for out_taps, place in ((taps_b, tap == col), (taps_f, tap == FILT - col)):
-        line = lax.dot_general(
-            taps16, place.astype(F32).astype(BF16), over_rows, preferred_element_type=F32
-        )
+        line = jnp.dot(taps16, place.astype(F32).astype(BF16), preferred_element_type=F32)
         for g in range(groups):
             spread = jnp.broadcast_to(line[g : g + 1, :], (FILT, 2 * FILT))
             moved = pltpu.roll(spread, 0, 1, stride=1, stride_axis=0)
@@ -224,8 +275,10 @@
         m_ref[part, :] = new
         factor = jnp.exp2((old - new) * scale)
         probs = jnp.exp2((scores - new[:, 0:1]) * scale)
-        if probs.shape[1] == 2 * HD:
-            sums = probs[:, :HD] + probs[:, HD:]
+        if probs.shape[1] >= HD:
+            sums = probs[:, :HD]
+            for begin in range(HD, probs.shape[1], HD):
+                sums = sums + probs[:, begin : begin + HD]
         else:
             lane0 = lax.broadcasted_iota(jnp.int32, (size, HD), 1) == 0
             sums = jnp.where(lane0, jnp.sum(probs, axis=1, keepdims=True), 0.0)
@@ -248,7 +301,9 @@
         for copy in back:
             copy.wait_recv()
 
-    attend(0, rows, kv[me, 0], kv[me, 1], 0, True)
+    for load in loads[3:]:
+        load.wait()
+    attend(0, rows, kv[0, me], kv[1, me], 0, True)
     attend(FAR + count, NEAR, aft_kv[0], aft_kv[1], count, True)
 
     lane_group = lax.broadcasted_iota(jnp.int32, (1, HD), 1) // GROUP_CH
@@ -264,25 +319,50 @@
     near_rows = count + NEAR
     d_mixed = band_product(taps_b, win_b, groups, lane_group)
     dv32[...] = (d_mixed * kf[FILT : FILT + near_rows]).astype(BF16).astype(F32)
-    gv_ref[...] = taps_sum(dv32, 0, count, fw_ref[2], 1).astype(BF16)
+    stage[3] = taps_sum(dv32, 0, count, fw_ref[2], 1).astype(BF16)
+    stores = [
+        pltpu.make_async_copy(stage.at[i], packed_ref.at[i], out_sem.at[i]) for i in range(4)
+    ]
+    stores[3].start()
     dk32[...] = d_mixed
 
     @pl.when(core == 1)
     def _():
-        kv_copy(sibling, sibling, sib_send).wait_recv()
-        attend(0, rows, kv[sibling, 0], kv[sibling, 1], -count, True)
-
-    def remote(d, c):
-        same = me - 2 * d
-        other = sibling - 2 * d
-        kv_copy(same, sibling, fwd_send.at[d]).wait_recv()
-        kv_copy(same, sibling, fwd_send.at[d]).start()
-        attend(0, rows, kv[same, 0], kv[same, 1], (same - me) * count, True)
-        kv_copy(other, sibling, fwd_send.at[d]).wait_recv()
-        attend(0, rows, kv[other, 0], kv[other, 1], (other - me) * count, True)
+        for half in range(2):
+            kv_copy(half, sibling, sibling, sib_send.at[half]).wait_recv()
+        attend(0, rows, kv[0, sibling], kv[1, sibling], -count, True)
+
+    def bring(step):
+        earlier = source(step)
+        slot = 2 * earlier + core
+        for half in range(2):
+            kv_copy(half, slot, sibling, fwd_send.at[half, earlier]).wait_recv()
+            each_relay(half, earlier, lambda copy: copy.start())
+            kv_copy(half, slot, sibling, fwd_send.at[half, earlier]).start()
+
+    def use(step):
+        earlier = source(step)
+        slot = 2 * earlier + 1 - core
+        for half in range(2):
+            kv_copy(half, slot, sibling, fwd_send.at[half, earlier]).wait_recv()
+        keys = kv[0, pl.ds(2 * earlier, 2)].reshape(2 * count, HD)
+        values = kv[1, pl.ds(2 * earlier, 2)].reshape(2 * count, HD)
+        attend(0, rows, keys, values, (2 * earlier - me) * count, True)
+
+    @pl.when(chip > 0)
+    def _():
+        bring(0)
+
+    def remote(step, c):
+        bring(step)
+        use(step - 1)
         return c
 
-    lax.fori_loop(1, chip + 1, remote, 0)
+    lax.fori_loop(1, chip, remote, 0)
+
+    @pl.when(chip > 0)
+    def _():
+        use(chip - 1)
 
     total = jnp.sum(l_ref[...], axis=1, keepdims=True)
     attended = (acc_ref[...] / total).astype(BF16).astype(F32)
@@ -315,7 +395,7 @@
     mean_sq = lax.dot_general(
         whole,
         jnp.full((8, HD), 1.0 / (8 * width), F32),
-        over_rows,
+        (((0,), (0,)), ((), ())),
         precision=lax.Precision.HIGHEST,
         preferred_element_type=F32,
     )[0:rows]
@@ -325,11 +405,14 @@
     vf = taps_sum(x32, NEAR, ext, fw_ref[2], -1).astype(BF16).astype(F32)
     win_f[0:ext, :] = (kf * vf).astype(BF16)
     signal = band_product(taps_f, win_f, groups, lane_group)
-    out_ref[...] = (qf[0:count] * signal[0:count]).astype(BF16)
+    stage[0] = (qf[0:count] * signal[0:count]).astype(BF16)
+    stores[0].start()
     dq32[...] = (cot_ext[0:near_rows, :].astype(F32) * signal).astype(BF16).astype(F32)
-    gq_ref[...] = taps_sum(dq32, 0, count, fw_ref[0], 1).astype(BF16)
+    stage[1] = taps_sum(dq32, 0, count, fw_ref[0], 1).astype(BF16)
+    stores[1].start()
     dk32[...] = (dk32[...] * vf[FILT : FILT + near_rows]).astype(BF16).astype(F32)
-    gk_ref[...] = taps_sum(dk32, 0, count, fw_ref[1], 1).astype(BF16)
+    stage[2] = taps_sum(dk32, 0, count, fw_ref[1], 1).astype(BF16)
+    stores[2].start()
 
     @pl.when(me < n - 1)
     def _():
@@ -343,21 +426,39 @@
 
     @pl.when(core == 0)
     def _():
-        kv_copy(me, sibling, sib_send).wait_send()
-
-    def sent_own(d, c):
-        kv_copy(me, me + 2 * d, kv_send.at[d]).wait_send()
+        for half in range(2):
+            kv_copy(half, me, sibling, sib_send.at[half]).wait_send()
+
+    each_own(lambda copy: copy.wait_send())
+
+    def sent_on(earlier, c):
+        for half in range(2):
+            kv_copy(half, 2 * earlier + core, sibling, fwd_send.at[half, earlier]).wait_send()
+            each_relay(half, earlier, lambda copy: copy.wait_send())
         return c
 
-    lax.fori_loop(1, chips - chip, sent_own, 0)
-
-    def sent_on(d, c):
-        kv_copy(me - 2 * d, sibling, fwd_send.at[d]).wait_send()
-        return c
-
-    lax.fori_loop(1, chip + 1, sent_on, 0)
+    lax.fori_loop(0, chip, sent_on, 0)
     for d in range(1, heads):
         sq_copy(d).wait_send()
+    for store in stores:
+        store.wait()
+
+
+def unpack(packed_ref, out_ref, gq_ref, gk_ref, gv_ref, stage, in_sems, sems):
+    loads = [
+        pltpu.make_async_copy(packed_ref.at[i], stage.at[i], in_sems.at[i]) for i in range(4)
+    ]
+    copies = [
+        pltpu.make_async_copy(stage.at[i], dst, sems.at[i])
+        for i, dst in enumerate((out_ref, gq_ref, gk_ref, gv_ref))
+    ]
+    for load in loads:
+        load.start()
+    for load, copy in zip(loads, copies):
+        load.wait()
+        copy.start()
+    for copy in copies:
+        copy.wait()
 
 
 def per_device(q_att, k_att, v_att, norm_gain, hy_q, hy_k, feat_w, mr_filt, cotangent):
@@ -365,18 +466,19 @@
     n = lax.axis_size("ctx")
     heads = lax.axis_size("head")
     groups = mr_filt.shape[1]
+    depth = feat_w.shape[0]
     rows = FAR + count + NEAR
     block = jax.ShapeDtypeStruct((count, channels), BF16)
-    vmem = pl.BlockSpec(memory_space=pltpu.VMEM)
     dma = pltpu.SemaphoreType.DMA
     near_rows = count + NEAR
-    return pl.pallas_call(
+    hbm = pl.BlockSpec(memory_space=pltpu.HBM)
+    packed = pl.pallas_call(
         functools.partial(kernel, n, heads, channels * heads),
-        out_shape=(block,) * 4,
-        in_specs=[vmem] * 9,
-        out_specs=(vmem,) * 4,
+        out_shape=jax.ShapeDtypeStruct((4, count, channels), BF16),
+        in_specs=[hbm] * 9,
+        out_specs=hbm,
         scratch_shapes=[
-            pltpu.VMEM((n, 2, count, HD), BF16),
+            pltpu.VMEM((2, n, count, HD), BF16),
             pltpu.VMEM((rows, HD), BF16),
             pltpu.VMEM((2, NEAR, HD), BF16),
             pltpu.VMEM((rows, HD), BF16),
@@ -395,19 +497,34 @@
             pltpu.VMEM((near_rows, HD), F32),
             pltpu.VMEM((near_rows, HD), F32),
             pltpu.VMEM((near_rows, HD), F32),
+            pltpu.VMEM((1, HD), F32),
+            pltpu.VMEM((depth, FEAT, HD), F32),
+            pltpu.VMEM((groups, FILT), F32),
+            pltpu.VMEM((4, count, HD), BF16),
+            dma((9,)),
+            dma((4,)),
             dma((9,)),
             dma((9,)),
-            dma((n // 2,)),
-            dma((n // 2,)),
-            dma((n,)),
-            dma,
+            dma((2, n // 2)),
+            dma((2, n // 2)),
+            dma((2,)),
+            dma((2, n)),
+            dma((2,)),
             dma((heads,)),
             dma((heads,)),
         ],
         compiler_params=pltpu.CompilerParams(
-            collective_id=0, has_side_effects=True, vmem_limit_bytes=40 * 1024 * 1024
+            collective_id=0, has_side_effects=True, vmem_limit_bytes=63 * 1024 * 1024
         ),
-    )(q_att, k_att, v_att, norm_gain.reshape(1, channels), hy_q, hy_k, feat_w, mr_filt, cotangent)
+    )(q_att, k_att, v_att, norm_gain.reshape(1, channels), hy_q, hy_k, feat_w, mr_filt.T, cotangent)
+    return pl.pallas_call(
+        unpack,
+        out_shape=(block,) * 4,
+        in_specs=[hbm],
+        out_specs=(hbm,) * 4,
+        scratch_shapes=[pltpu.VMEM((4, count, channels), BF16), dma((4,)), dma((4,))],
+        compiler_params=pltpu.CompilerParams(vmem_limit_bytes=63 * 1024 * 1024),
+    )(packed)
 
 
 def solution(mesh):

time: 30 us -> 23.2 us (0.77); the launches traced: 29.4 us -> 23 us
  local copies, waits for them, and re-layouts: 8.24 us -> 0 us
  Pallas kernels: 20.5 us -> 22.4 us
    unnamed x21 -> x0, local copies, waits for them, and re-layouts: 8.24 us -> none
    pallas_call x0 -> x1, Pallas kernels: none -> 1.63 us  [per_device(): pl.pallas_call(unpack, out_shape=(block,) * 4, in_specs=[hbm], out_specs=...]
where the time goes in v2:
time: 23.2 us; the launch traced here: 23 us
  Pallas kernels  22.4 us (97%)
  between operations  0.64 us (3%)
    pallas_call x1, Pallas kernels, per_device(): pl.pallas_call(functools.partial(kernel, n, heads, channels * heads), out...  20.7 us
    pallas_call x1, Pallas kernels, per_device(): pl.pallas_call(unpack, out_shape=(block,) * 4, in_specs=[hbm], out_specs=...  1.63 us

profile of v2, /device:TPU:6, one launch (start us, length us, event | category | flops | bytes accessed | tf_op | source)
XLA Modules:
  0.0 23.0 jit_solution(18161089974959654502)
XLA Ops:
  0.6 20.7 %shard_map.120.packed_ref = bf16[4,256,128]{2,1,0:T(8,128)(2,1)} custom-call(bf16[256,128]{1,0:T(8,128)(2,1)} %q_ref.1, bf16[256,128]{1,0:T(8,128)(2,1)} %k_ref.1, bf16[256,128]{1,0:T(8,128)(2,1)} %v_ref.1, f32[1,128]{1,0:T(1,128)} %bitcast.3, bf16[256,128]{1,0:T(8,128)(2,1)} %hyq_ref.1, bf16[256,128]{1,0:T(8,128)(2,1)} %hyk_ref.1, f32[3,7,128]{2,1,0:T(8,128)} %fw_hbm.1, ...), custom_call_target="tpu_custom_call" | custom-call | tf_op jit(solution)/shard_map/pallas_call | solution.py:475
  21.4 1.6 %shard_map.121 = (bf16[256,128]{1,0:T(8,128)(2,1)}, bf16[256,128]{1,0:T(8,128)(2,1)}, bf16[256,128]{1,0:T(8,128)(2,1)}, bf16[256,128]{1,0:T(8,128)(2,1)}) custom-call(bf16[4,256,128]{2,1,0:T(8,128)(2,1)} %shard_map.120.packed_ref), custom_call_target="tpu_custom_call" | custom-call | tf_op jit(solution)/shard_map/pallas_call | solution.py:520

commit v3 on v2

--- a/solution.py
+++ b/solution.py
@@ -366,14 +366,14 @@
 
     total = jnp.sum(l_ref[...], axis=1, keepdims=True)
     attended = (acc_ref[...] / total).astype(BF16).astype(F32)
-    squares[head] = jnp.zeros((8, 512), F32)
+    squares[head] = jnp.zeros((1, 512), F32)
     squares[head, :, 0:rows] = lax.dot_general(
         jnp.ones((8, HD), F32),
         attended * attended,
         over_last,
         precision=lax.Precision.HIGHEST,
         preferred_element_type=F32,
-    )
+    )[0:1]
 
     def sq_copy(d):
         return pltpu.make_async_remote_copy(
@@ -393,7 +393,7 @@
     for other in range(1, heads):
         whole = whole + squares[other]
     mean_sq = lax.dot_general(
-        whole,
+        jnp.broadcast_to(whole, (8, 512)),
         jnp.full((8, HD), 1.0 / (8 * width), F32),
         (((0,), (0,)), ((), ())),
         precision=lax.Precision.HIGHEST,
@@ -484,7 +484,7 @@
             pltpu.VMEM((rows, HD), BF16),
             pltpu.VMEM((rows, HD), BF16),
             pltpu.VMEM((count + FAR, HD), BF16),
-            pltpu.VMEM((heads, 8, 512), F32),
+            pltpu.VMEM((heads, 1, 512), F32),
             pltpu.VMEM((groups * FILT, 2 * FILT), BF16),
             pltpu.VMEM((groups * FILT, 2 * FILT), BF16),
             pltpu.VMEM((512, HD), BF16),

time: 23.2 us -> 23 us (level)
  no operation moved by 1% of the time
where the time goes in v3:
time: 23 us; the launch traced here: 22.8 us
  Pallas kernels  22.2 us (97%)
  between operations  0.64 us (3%)
    pallas_call x1, Pallas kernels, per_device(): pl.pallas_call(functools.partial(kernel, n, heads, channels * heads), out...  20.5 us
    pallas_call x1, Pallas kernels, per_device(): pl.pallas_call(unpack, out_shape=(block,) * 4, in_specs=[hbm], out_specs=...  1.63 us

profile of v3, /device:TPU:6, one launch (start us, length us, event | category | flops | bytes accessed | tf_op | source)
XLA Modules:
  0.0 22.8 jit_solution(6710744928058986589)
XLA Ops:
  0.6 20.5 %shard_map.120.packed_ref = bf16[4,256,128]{2,1,0:T(8,128)(2,1)} custom-call(bf16[256,128]{1,0:T(8,128)(2,1)} %q_ref.1, bf16[256,128]{1,0:T(8,128)(2,1)} %k_ref.1, bf16[256,128]{1,0:T(8,128)(2,1)} %v_ref.1, f32[1,128]{1,0:T(1,128)} %bitcast.3, bf16[256,128]{1,0:T(8,128)(2,1)} %hyq_ref.1, bf16[256,128]{1,0:T(8,128)(2,1)} %hyk_ref.1, f32[3,7,128]{2,1,0:T(8,128)} %fw_hbm.1, ...), custom_call_target="tpu_custom_call" | custom-call | tf_op jit(solution)/shard_map/pallas_call | solution.py:475
  21.2 1.6 %shard_map.121 = (bf16[256,128]{1,0:T(8,128)(2,1)}, bf16[256,128]{1,0:T(8,128)(2,1)}, bf16[256,128]{1,0:T(8,128)(2,1)}, bf16[256,128]{1,0:T(8,128)(2,1)}) custom-call(bf16[4,256,128]{2,1,0:T(8,128)(2,1)} %shard_map.120.packed_ref), custom_call_target="tpu_custom_call" | custom-call | tf_op jit(solution)/shard_map/pallas_call | solution.py:520
